TPU v7x, 512 devices: a whole 4x4x16 slice. The times are simulated.
512 devices in a mesh: docs: 64 (over y, z), dim: 8 (over x, core).
Axes of the slice: x: 4, y: 4, z: 16, core: 2. Of those that a mesh axis runs over, the one named last changes fastest.
Arguments:
- sketches: bfloat16 [32768, 8192], P('docs', 'dim'), may hold values from -1.5 to 1.5
- clusters: int32 [32768], P('docs'), may hold values from 0 to 4095, as said below
- queries: bfloat16 [1024, 8192], P(None, 'dim'), may hold values from -6 to 6
Outputs:
- gram: float32 [4096, 4096], P(('docs', 'dim'))
- scores: float32 [4096, 1024], P(('docs', 'dim'))
Inputs may be any that keep to these rules, and one draw needn't show every extreme that they name: Cluster c is owned by docs index c // 64. Among the documents of one index of docs (aligned blocks of 512), at most 32 belong to clusters of one owner, and in every block some owner gets exactly 32.
All inputs are finite; a program needn't handle non-finite values.
Results may differ from a plain program's by a relative error of at most 0.0029.
Values may be sent and summed in bfloat16 or wider, within the bound.
A program may use at most 64 MiB of HBM per device.

v0:
```python
import jax
import jax.numpy as jnp
from jax import lax
from jax.sharding import PartitionSpec as P

K = 8192
CL_DEV = 64


def outer_panel(own_rows, scale, piece):
    product = lax.dot_general(
        own_rows, piece, (((1,), (1,)), ((), ())), preferred_element_type=jnp.float32
    )
    return product * scale


def per_device(sketches, clusters, queries):
    owners_count = lax.axis_size("docs")
    doc_rows = sketches.shape[0]
    capacity = max(2, 4 * doc_rows // owners_count)
    owner = clusters // CL_DEV
    local_index = clusters % CL_DEV
    position = jnp.arange(doc_rows, dtype=jnp.int32)
    same_owner = owner[:, None] == owner[None, :]
    earlier = position[:, None] > position[None, :]
    rank = jnp.sum((same_owner & earlier).astype(jnp.int32), axis=1)
    position_count = owners_count * capacity
    slot = owner * capacity + rank
    slot_doc = jnp.zeros((position_count,), jnp.int32).at[slot].set(position)
    slot_cluster = jnp.full((position_count,), -1, jnp.int32).at[slot].set(local_index)
    send_rows = jnp.take(sketches, slot_doc, axis=0).reshape(
        owners_count, capacity, sketches.shape[1]
    )
    send_ids = slot_cluster.reshape(owners_count, capacity)
    got_rows, got_ids = (
        lax.all_to_all(send_rows, "docs", split_axis=0, concat_axis=0, tiled=True),
        lax.all_to_all(send_ids, "docs", split_axis=0, concat_axis=0, tiled=True),
    )
    got_rows = got_rows.reshape(position_count, sketches.shape[1])
    got_ids = got_ids.reshape(position_count)
    onehot = (got_ids[None, :] == jnp.arange(CL_DEV, dtype=jnp.int32)[:, None]).astype(jnp.bfloat16)
    own_sums = jnp.dot(onehot, got_rows, preferred_element_type=jnp.float32).astype(jnp.bfloat16)
    score_scale = K ** (-0.5)
    query_terms = (
        lax.dot_general(
            own_sums, queries, (((1,), (1,)), ((), ())), preferred_element_type=jnp.float32
        )
        * score_scale
    )
    gram_terms = outer_panel(
        own_sums, 1.0 / K, lax.all_gather(own_sums, "docs", axis=0, tiled=True)
    )
    gram, scores = (
        lax.psum_scatter(gram_terms, "dim", scatter_dimension=0, tiled=True),
        lax.psum_scatter(query_terms, "dim", scatter_dimension=0, tiled=True),
    )
    return (gram, scores)


def solution(mesh):
    in_specs = (P("docs", "dim"), P("docs"), P(None, "dim"))
    out_specs = (P(("docs", "dim"), None), P(("docs", "dim"), None))
    return jax.shard_map(
        per_device, mesh=mesh, in_specs=in_specs, out_specs=out_specs, check_vma=False
    )
```

profile of v0, /device:TPU:1, one launch (start us, length us, event | category | flops | bytes accessed | tf_op | source)
XLA Modules:
  0.0 454.7 jit_solution(15812697730806128349)
XLA Ops:
  8.0 0.0 copy-start
  8.0 0.8 add_select_fusion
  8.9 0.3 convert_reduce_fusion
  9.1 2.5 scatter_custom_fusion
  11.6 0.7 all_to_all.9
  12.3 19.3 %all-to-all-start = ((s32[64,1,32]{2,1,0:T(1,128)}), s32[64,1,32]{2,1,0:T(1,128)S(1)}, u32[]{:S(2)}, u32[]{:S(2)}) async-start(s32[64,1,32]{2,1,0:T(1,128)} %bitcast), calls=%async_computation | async-start | bytes 65536 | tf_op jit(solution)/shard_map/all_to_all | solution.py:37
  31.6 2.5 scatter_custom_fusion.1
  34.0 0.1 broadcast_in_dim.32
  34.1 12.3 %gather_fusion = bf16[2048,1024]{1,0:T(8,128)(2,1)} fusion(bf16[512,1024]{1,0:T(8,128)(2,1)} %param.3, s32[2048]{0:T(1024)S(1)} %fusion.2), kind=kCustom, calls=%fused_computation | custom fusion | bytes 8396800 | tf_op jit(solution)/shard_map/jit(_take)/gather | solution.py:31
  46.5 3.8 broadcast_select_fusion
  50.3 0.0 all-to-all-done
  50.3 14.8 %all-to-all-start.1 = ((bf16[64,32,1024]{2,1,0:T(8,128)(2,1)}), bf16[64,32,1024]{2,1,0:T(8,128)(2,1)}, u32[]{:S(2)}, u32[]{:S(2)}) async-start(bf16[64,32,1024]{2,1,0:T(8,128)(2,1)} %broadcast_select_fusion), calls=%async_computation.1 | async-start | bytes 8388608 | tf_op jit(solution)/shard_map/all_to_all | solution.py:36
  65.1 0.0 all-gather.2.cloned.1.call-start
  65.2 0.5 broadcast.45
  65.7 0.7 reduce.3
  66.4 0.1 eq.33
  66.5 180.7 %all-to-all-done.1 = bf16[64,32,1024]{2,1,0:T(8,128)(2,1)} async-done(((bf16[64,32,1024]{2,1,0:T(8,128)(2,1)}), bf16[64,32,1024]{2,1,0:T(8,128)(2,1)}, u32[]{:S(2)}, u32[]{:S(2)}) %all-to-all-start.1) | async-done | bytes 4194336 | tf_op jit(solution)/shard_map/all_to_all | solution.py:36
  247.2 3.7 convolution_convert_fusion
  250.9 0.0 all-gather.2.cloned.1.call-update
  250.9 0.0 reduce-scatter.5.cloned.1.call-start
  251.0 0.0 copy-done
  251.0 2.4 convolution_multiply_fusion.1
  253.4 0.0 reduce-scatter.5.cloned.1.call-update
  253.4 0.0 reduce-scatter.3.cloned.1.call-start
  253.4 146.1 %all-gather.2.cloned.1.call-done = bf16[4096,1024]{1,0:T(8,128)(2,1)} async-done(((bf16[64,1024]{1,0:T(8,128)(2,1)}), bf16[4096,1024]{1,0:T(8,128)(2,1)}) %all-gather.2.cloned.1.call-update) | async-done | bytes 8388624 | tf_op jit(solution)/shard_map/all_gather | solution.py:51
  399.6 7.2 %convolution_multiply_fusion = f32[64,4096]{1,0:T(8,128)} fusion(bf16[64,1024]{1,0:T(8,128)(2,1)} %convolution_convert_fusion, bf16[4096,1024]{1,0:T(8,128)(2,1)} %all-gather.2.cloned.1.call-done), kind=kOutput, calls=%fused_computation.3 | convolution fusion | flops 537133056 | bytes 9568256 | tf_op jit(solution)/shard_map/dot_general | solution.py:11
  406.8 0.0 reduce-scatter.3.cloned.1.call-update
  406.8 0.0 reduce-scatter.5.cloned.1.call-done
  406.8 40.4 %reduce-scatter.3.cloned.1.call-done = f32[8,4096]{1,0:T(8,128)} async-done(((f32[64,4096]{1,0:T(8,128)}), f32[8,4096]{1,0:T(8,128)}) %reduce-scatter.3.cloned.1.call-update) | async-done | bytes 131088 | tf_op jit(solution)/shard_map/reduce_scatter | solution.py:54
  (4 shorter events, 0.0 us)
Async XLA Ops:
  8.0 243.0 %copy-start = (bf16[1024,1024]{1,0:T(8,128)(2,1)S(1)}, bf16[1024,1024]{1,0:T(8,128)(2,1)}, u32[]{:S(2)}) copy-start(bf16[1024,1024]{1,0:T(8,128)(2,1)} %param.5) | copy-start | bytes 6291460
  12.3 38.0 %all-to-all-start = ((s32[64,1,32]{2,1,0:T(1,128)}), s32[64,1,32]{2,1,0:T(1,128)S(1)}, u32[]{:S(2)}, u32[]{:S(2)}) async-start(s32[64,1,32]{2,1,0:T(1,128)} %bitcast), calls=%async_computation | async-start | bytes 65536 | tf_op jit(solution)/shard_map/all_to_all | solution.py:37
  50.3 197.0 %all-to-all-start.1 = ((bf16[64,32,1024]{2,1,0:T(8,128)(2,1)}), bf16[64,32,1024]{2,1,0:T(8,128)(2,1)}, u32[]{:S(2)}, u32[]{:S(2)}) async-start(bf16[64,32,1024]{2,1,0:T(8,128)(2,1)} %broadcast_select_fusion), calls=%async_computation.1 | async-start | bytes 8388608 | tf_op jit(solution)/shard_map/all_to_all | solution.py:36
  65.1 334.5 %all-gather.2.cloned.1.call-start = ((), (), s32[]{:S(2)}) async-start(), calls=%async_computation.4 | async-start | bytes 8519680 | tf_op jit(solution)/shard_map/all_gather | solution.py:51
  250.9 155.9 %reduce-scatter.5.cloned.1.call-start = ((), (), s32[]{:S(2)}) async-start(), calls=%async_computation.6 | async-start | bytes 294912 | tf_op jit(solution)/shard_map/reduce_scatter | solution.py:55
  253.4 193.9 %reduce-scatter.3.cloned.1.call-start = ((), (), s32[]{:S(2)}) async-start(), calls=%async_computation.5 | async-start | bytes 1179648 | tf_op jit(solution)/shard_map/reduce_scatter | solution.py:54
Sparse Core Ops, SparseCore 0:
  251.1 148.4 all-gather.1
Sparse Core Ops, SparseCore 1:
  254.8 36.1 reduce-scatter.4
  406.9 40.3 reduce-scatter.2
where the time goes:
time: 456 us; the launch traced here: 455 us
  waiting for transfers between devices  367 us (80%)
  starting transfers between devices  34.2 us (8%)
  local copies, waits for them, and re-layouts  18.6 us (4%)
  between operations  15.6 us (3%)
  matrix products  13.3 us (3%)
  other arithmetic  5.63 us (1%)
    all_to_all x1, waiting for transfers between devices, per_device(): lax.all_to_all(send_rows, 'docs', split_axis=0, concat_axis=0, tiled=True)  181 us
    all_gather x1, waiting for transfers between devices, per_device(): lax.all_gather(own_sums, 'docs', axis=0, tiled=True)  146 us
    reduce_scatter x1, waiting for transfers between devices, per_device(): lax.psum_scatter(gram_terms, 'dim', scatter_dimension=0, tiled=True)  40.4 us
    all_to_all x1, starting transfers between devices, per_device(): lax.all_to_all(send_ids, 'docs', split_axis=0, concat_axis=0, tiled=True)  19.3 us
    all_to_all x1, starting transfers between devices, per_device(): lax.all_to_all(send_rows, 'docs', split_axis=0, concat_axis=0, tiled=True)  14.8 us
    gather x1, local copies, waits for them, and re-layouts, per_device(): jnp.take(sketches, slot_doc, axis=0)  12.3 us
  transfers between devices with their start and end apart: 5, of which 3 were waited for; matrix products, arithmetic and copies ran while one was open for 7% of the time, Pallas kernels for 0%

commit v1 on v0

v1 whole, which is shorter than its diff:
```python
import functools
import math

import jax
import jax.numpy as jnp
from jax import lax
from jax.experimental import pallas as pl
from jax.experimental.pallas import tpu as pltpu
from jax.sharding import PartitionSpec as P

MESH = pl.DeviceIdType.MESH
CL = 64
NY = 4
LN2 = math.log(2.0)
BITS = 15


def power(level):
    return jnp.exp(level * LN2).astype(jnp.bfloat16).astype(jnp.float32)


def quantise(part):
    peak = jnp.maximum(jnp.max(jnp.abs(part), axis=0, keepdims=True), 1e-30)
    level = jnp.floor(jnp.log(peak) * (1.0 / LN2) + 0.001) + 1.0
    values = jnp.round(part * power(BITS - level)).astype(jnp.int32).astype(jnp.int16)
    levels = jnp.broadcast_to(level, (16, part.shape[1])).astype(jnp.int32).astype(jnp.int16)
    return values, levels


def restore(values, levels):
    level = levels.astype(jnp.int32).astype(jnp.float32)[0:1]
    return values.astype(jnp.int32).astype(jnp.float32) * power(level - BITS)


def kernel(
    sizes, sk_ref, ids_ref, qu_ref, gram_ref, scores_ref,
    docs_in, ids_in, quer, zpos, row, acc, rs_out, rs_in, own_cols, cols, rows,
    part, pair_in, half, x_in, done, y_in, s_part, s_pair_in, s_half, s_x_in,
    local_sem, a_ss, a_rs, i_ss, i_rs, rs_ss, rs_rs, c_ss, c_rs, r_ss, r_rs, g_ss, g_rs,
    p_ss, p_rs, x_ss, x_rs, f_ss, f_rs, sp_ss, sp_rs, sx_ss, sx_rs,
):
    ny, nz, nx, cl = sizes
    n_docs, kd = sk_ref.shape
    kq = kd // ny
    sub = kq // 2
    n_rows = ny * cl
    hops = nz // 2
    groups = nz // 2
    dims = 2 * nx

    docs_at = lax.axis_index("docs")
    dim_at = lax.axis_index("dim")
    y, z = docs_at // nz, docs_at % nz
    x, core = dim_at // 2, dim_at % 2

    def dev(yy, zz, xx, cc):
        return (yy * nz + zz, xx * 2 + cc)

    def y_peer(o):
        return dev((y + o) % ny, z, x, core)

    def x_peer(o):
        return dev(y, z, (x + o) % nx, core)

    z_next = (dev(y, (z + 1) % nz, x, core), dev(y, (z + nz - 1) % nz, x, core))
    mate = dev(y, z, x, 1 - core)

    def remote(src, dst, ssem, rsem, to):
        return pltpu.make_async_remote_copy(
            src_ref=src, dst_ref=dst, send_sem=ssem, recv_sem=rsem, device_id=to, device_id_type=MESH
        )

    own_docs = pltpu.make_async_copy(
        sk_ref.at[:, pl.ds(pl.multiple_of(y * kq, kq), kq)], docs_in.at[0], local_sem.at[0]
    )
    own_docs.start()
    own_quer = pltpu.make_async_copy(qu_ref, quer, local_sem.at[1])
    own_quer.start()

    barrier = pltpu.get_barrier_semaphore()
    partners = [y_peer(o) for o in range(1, ny)] + [x_peer(o) for o in range(1, nx)] + list(z_next) + [mate]
    for to in partners:
        pl.semaphore_signal(barrier, inc=1, device_id=to, device_id_type=MESH)
    pl.semaphore_wait(barrier, len(partners))

    def ids_copy(o):
        return remote(ids_ref, ids_in.at[o], i_ss.at[o], i_rs.at[o], y_peer(o))

    def docs_copy(o, h):
        at = pl.multiple_of(((y + o) % ny) * kq + h * sub, sub)
        return remote(
            sk_ref.at[:, pl.ds(at, sub)], docs_in.at[o, :, pl.ds(h * sub, sub)], a_ss.at[o, h], a_rs.at[o, h], y_peer(o)
        )

    for o in range(1, ny):
        ids_copy(o).start()
    for h in range(2):
        for o in range(1, ny):
            docs_copy(o, h).start()
    ids_in[0] = ids_ref[...]
    for o in range(1, ny):
        ids_copy(o).wait_recv()
    ids = ids_in[...]
    owner = lax.shift_right_logical(ids, int(math.log2(cl)))
    zpos[...] = lax.bitwise_and(owner, nz - 1)
    row[...] = lax.shift_right_logical(owner, int(math.log2(nz))) * cl + lax.bitwise_and(ids, cl - 1)
    own_docs.wait()
    for h in range(2):
        for o in range(1, ny):
            docs_copy(o, h).wait_recv()

    def onehot(target):
        places = lax.broadcasted_iota(jnp.int32, (n_rows, n_docs), 0)
        pieces = []
        for o in range(ny):
            here = jnp.where(zpos[o, 0:1, :] == target, row[o, 0:1, :], -1)
            pieces.append((here == places).astype(jnp.float32).astype(jnp.bfloat16))
        return jnp.concatenate(pieces, axis=1)

    def sums(targets):
        hot = [onehot(t) for t in targets]
        hot = jnp.concatenate(hot, axis=0) if len(hot) > 1 else hot[0]
        return jnp.dot(hot, docs_in[...].reshape(ny * n_docs, kq), preferred_element_type=jnp.float32)

    def rs_copy(way, h, s):
        return remote(
            rs_out.at[way, h, s], rs_in.at[way, h, s], rs_ss.at[way, h, s], rs_rs.at[way, h, s], z_next[way]
        )

    def rs_send(way, h, s, value):
        values, levels = quantise(value)
        rs_out[way, h, s, 0:n_rows] = values
        rs_out[way, h, s, n_rows : n_rows + 16] = levels
        rs_copy(way, h, s).start()

    def rs_got(way, h, s):
        rs_copy(way, h, s).wait_recv()
        return restore(rs_in[way, h, s, 0:n_rows], rs_in[way, h, s, n_rows : n_rows + 16])

    def fill(s):
        both = sums([(z + hops - s) % nz, (z + nz - hops + s) % nz])
        acc[0] = both[:n_rows]
        acc[1] = both[n_rows:]

    def mine(way, h):
        return acc[way, :, h * sub : (h + 1) * sub]

    far = sums([(z + hops) % nz])
    rs_send(0, 0, 0, far[:, :sub])
    rs_send(1, 1, 0, far[:, sub:])
    fill(1)
    rs_send(0, 1, 1, mine(0, 1))
    rs_send(1, 0, 1, mine(1, 0))
    rs_send(0, 0, 1, mine(0, 0) + rs_got(0, 0, 0))
    rs_send(1, 1, 1, mine(1, 1) + rs_got(1, 1, 0))
    fill(2)

    def rs_step(s, carry):
        for h in range(2):
            for way in range(2):
                rs_send(way, h, s, mine(way, h) + rs_got(way, h, s - 1))
        fill(s + 1)
        return carry

    lax.fori_loop(2, hops, rs_step, 0)
    last = hops - 1
    own = jnp.concatenate(
        [mine(0, h) + rs_got(0, h, last) + rs_got(1, h, last) for h in range(2)], axis=1
    )

    own_cols[...] = own.astype(jnp.bfloat16).reshape(ny, cl, kq)
    order = own.reshape(ny, nx, 2, 8, kq)
    rows[0] = jnp.concatenate(
        [order[yy, xx, cc] for cc in range(2) for xx in range(nx) for yy in range(ny)], axis=0
    ).astype(jnp.bfloat16)

    def c_copy(o):
        return remote(own_cols.at[(y + o) % ny], cols.at[0, o], c_ss.at[o], c_rs.at[o], y_peer(o))

    def r_copy(o):
        return remote(rows.at[0], rows.at[o], r_ss.at[o], r_rs.at[o], y_peer(o))

    for o in range(1, ny):
        c_copy(o).start()
    for o in range(1, ny):
        r_copy(o).start()
    cols[0, 0] = own_cols[y]

    hq = ny // 2

    def g_copy(way, h, d):
        if way == 0:
            src, dst = (nz - d + 1) % nz, nz - d
        else:
            src, dst = d - 1, d
        return remote(
            cols.at[src, pl.ds(h * hq, hq)], cols.at[dst, pl.ds(h * hq, hq)],
            g_ss.at[way, h, d - 1], g_rs.at[way, h, d - 1], z_next[way],
        )

    for h in range(2):
        for o in range(max(1, h * hq), (h + 1) * hq):
            c_copy(o).wait_recv()
        for way in range(2):
            g_copy(way, h, 1).start()

    own_quer.wait()
    total = None
    for q in range(ny):
        at = pl.multiple_of(((y + ny - q) % ny) * kq, kq)
        term = lax.dot_general(
            cols[0, q], quer[:, pl.ds(at, kq)], (((1,), (1,)), ((), ())), preferred_element_type=jnp.float32
        )
        total = term if total is None else total + term
    total = total.reshape(nx, 2, 8, total.shape[1])
    for cc in range(2):
        for xx in range(nx):
            s_part[cc, xx] = total[xx, cc]

    def sp_copy():
        return remote(s_part.at[1 - core], s_pair_in, sp_ss.at[0], sp_rs.at[0], mate)

    def sx_copy(o):
        return remote(s_half.at[(x + o) % nx], s_x_in.at[o], sx_ss.at[o], sx_rs.at[o], x_peer(o))

    sp_copy().start()
    for o in range(1, ny):
        r_copy(o).wait_recv()

    def block(d, g):
        first = (d % 2) * (d - 1) + (1 - d % 2) * (nz - d)
        total = None
        for q in range(ny):
            pair = cols[pl.ds(first, 2), q].reshape(2 * cl, kq)
            term = lax.dot_general(
                rows[q], pair, (((1,), (1,)), ((), ())), preferred_element_type=jnp.float32
            )
            total = term if total is None else total + term
        part[g] = total.reshape(2, nx, ny, 8, 2 * cl)

    def p_copy(g):
        return remote(part.at[g, 1 - core], pair_in.at[g], p_ss.at[g], p_rs.at[g], mate)

    def x_copy(g, o):
        return remote(half.at[g, (x + o) % nx], x_in.at[g, o], x_ss.at[g, o], x_rs.at[g, o], x_peer(o))

    def pair_sum(g):
        p_copy(g).wait_recv()
        half[g] = part[g, core] + pair_in[g]
        for o in range(1, nx):
            x_copy(g, o).start()

    def x_sum(g):
        d = g + 1
        first = (d % 2) * (d - 1) + (1 - d % 2) * (nz - d)
        total = half[g, x]
        for o in range(1, nx):
            x_copy(g, o).wait_recv()
            total = total + x_in[g, o]
        at = first // 2
        for yy in range(ny):
            done[yy, at] = total[yy]

    def gather_step(d, carry):
        for h in range(2):
            for way in range(2):
                g_copy(way, h, d).wait_recv()
                g_copy(way, h, d + 1).start()
        block(d, d - 1)
        p_copy(d - 1).start()

        @pl.when(d >= 2)
        def _():
            pair_sum(d - 2)

        @pl.when(d >= 3)
        def _():
            x_sum(d - 3)

        return carry

    lax.fori_loop(1, hops - 1, gather_step, 0)
    d = hops - 1
    for h in range(2):
        for way in range(2):
            g_copy(way, h, d).wait_recv()
            if way == h:
                g_copy(way, h, d + 1).start()
    block(d, d - 1)
    p_copy(d - 1).start()
    pair_sum(d - 2)
    x_sum(d - 3)
    sp_copy().wait_recv()
    s_half[...] = s_part[core] + s_pair_in[...]
    for o in range(1, nx):
        sx_copy(o).start()
    d = hops
    for h in range(2):
        g_copy(h, h, d).wait_recv()
    block(d, d - 1)
    p_copy(d - 1).start()
    pair_sum(d - 2)
    x_sum(d - 3)
    total = s_half[x]
    for o in range(1, nx):
        sx_copy(o).wait_recv()
        total = total + s_x_in[o]
    scores_ref[...] = total * ((kd * dims) ** -0.5)
    pair_sum(d - 1)
    x_sum(d - 2)
    x_sum(d - 1)

    def f_copy(o):
        return remote(done.at[(y + o) % ny], y_in.at[o], f_ss.at[o], f_rs.at[o], y_peer(o))

    for o in range(1, ny):
        f_copy(o).start()
    width = nz * cl
    for o in range(ny):
        if o:
            f_copy(o).wait_recv()
            got = y_in[o]
        else:
            got = done[y]
        wide = jnp.concatenate([got[g] for g in range(groups)], axis=1) * (1.0 / (kd * dims))
        at = pl.multiple_of(((y + ny - o) % ny) * width, width)
        gram_ref[:, pl.ds(at, width)] = pltpu.roll(wide, z * cl, 1)

    for o in range(1, ny):
        ids_copy(o).wait_send()
        for h in range(2):
            docs_copy(o, h).wait_send()
        c_copy(o).wait_send()
        r_copy(o).wait_send()
        f_copy(o).wait_send()
    sp_copy().wait_send()
    for o in range(1, nx):
        sx_copy(o).wait_send()
    rs_copy(0, 0, 0).wait_send()
    rs_copy(1, 1, 0).wait_send()
    g_copy(0, 0, hops).wait_send()
    g_copy(1, 1, hops).wait_send()

    def drain(s, carry):
        for way in range(2):
            for h in range(2):
                rs_copy(way, h, s).wait_send()
                g_copy(way, h, s).wait_send()
        return carry

    lax.fori_loop(1, hops, drain, 0)

    def drain_sums(g, carry):
        p_copy(g).wait_send()
        for o in range(1, nx):
            x_copy(g, o).wait_send()
        return carry

    lax.fori_loop(0, groups, drain_sums, 0)


def per_device(ny, cl, sketches, clusters, queries):
    nz = lax.axis_size("docs") // ny
    nx = lax.axis_size("dim") // 2
    n_docs, kd = sketches.shape
    nq = queries.shape[0]
    kq, rows, hops, groups = kd // ny, ny * cl, nz // 2, nz // 2
    ids = jnp.broadcast_to(clusters[None, :], (8, n_docs))
    f32, bf16, i32, i16 = jnp.float32, jnp.bfloat16, jnp.int32, jnp.int16
    vmem, dma = pltpu.VMEM, pltpu.SemaphoreType.DMA
    whole = pl.BlockSpec(memory_space=pltpu.VMEM)
    away = pl.BlockSpec(memory_space=pl.ANY)
    return pl.pallas_call(
        functools.partial(kernel, (ny, nz, nx, cl)),
        out_shape=(
            jax.ShapeDtypeStruct((8, ny * nz * cl), f32),
            jax.ShapeDtypeStruct((8, nq), f32),
        ),
        in_specs=[away, whole, away],
        out_specs=(whole, whole),
        scratch_shapes=[
            vmem((ny, n_docs, kq), bf16),
            vmem((ny, 8, n_docs), i32),
            vmem((nq, kd), bf16),
            vmem((ny, 8, n_docs), i32),
            vmem((ny, 8, n_docs), i32),
            vmem((2, rows, kq), f32),
            vmem((2, 2, hops, rows + 16, kq // 2), i16),
            vmem((2, 2, hops, rows + 16, kq // 2), i16),
            vmem((ny, cl, kq), bf16),
            vmem((nz, ny, cl, kq), bf16),
            vmem((ny, rows, kq), bf16),
            vmem((groups, 2, nx, ny, 8, 2 * cl), f32),
            vmem((groups, nx, ny, 8, 2 * cl), f32),
            vmem((groups, nx, ny, 8, 2 * cl), f32),
            vmem((groups, nx, ny, 8, 2 * cl), f32),
            vmem((ny, groups, 8, 2 * cl), f32),
            vmem((ny, groups, 8, 2 * cl), f32),
            vmem((2, nx, 8, nq), f32),
            vmem((nx, 8, nq), f32),
            vmem((nx, 8, nq), f32),
            vmem((nx, 8, nq), f32),
            dma((2,)),
            dma((ny, 2)), dma((ny, 2)),
            dma((ny,)), dma((ny,)),
            dma((2, 2, hops)), dma((2, 2, hops)),
            dma((ny,)), dma((ny,)),
            dma((ny,)), dma((ny,)),
            dma((2, 2, hops)), dma((2, 2, hops)),
            dma((groups,)), dma((groups,)),
            dma((groups, nx)), dma((groups, nx)),
            dma((ny,)), dma((ny,)),
            dma((1,)), dma((1,)),
            dma((nx,)), dma((nx,)),
        ],
        compiler_params=pltpu.CompilerParams(
            collective_id=0, has_side_effects=True, vmem_limit_bytes=56 * 1024 * 1024
        ),
    )(sketches, ids, queries)


def solution(mesh, ny=NY, cl=CL):
    in_specs = (P("docs", "dim"), P("docs"), P(None, "dim"))
    out_specs = (P(("docs", "dim"), None), P(("docs", "dim"), None))
    return jax.shard_map(
        functools.partial(per_device, ny, cl), mesh=mesh, in_specs=in_specs, out_specs=out_specs, check_vma=False
    )
```

time: 456 us -> 114 us (0.25)
  waiting for transfers between devices: 367 us -> 0 us
  Pallas kernels: 0 us -> 108 us
  starting transfers between devices: 34.2 us -> 0 us
  between operations: 15.6 us -> 0.64 us
  local copies, waits for them, and re-layouts: 18.6 us -> 4.23 us
  matrix products: 13.3 us -> 0 us
  other arithmetic: 5.63 us -> 0 us
    all_to_all x2 -> x0, waiting for transfers between devices: 181 us -> none  [the longest x1 181 us: per_device(): lax.all_to_all(send_rows, 'docs', split_axis=0, concat_axis=0, tiled=True)]
    all_gather x1 -> x0, waiting for transfers between devices: 146 us -> none  [per_device(): lax.all_gather(own_sums, 'docs', axis=0, tiled=True)]
    pallas_call x0 -> x1, Pallas kernels: none -> 108 us  [per_device(): pl.pallas_call(functools.partial(kernel, (ny, nz, nx, cl)), out_shape=(ja...]
    reduce_scatter x2 -> x0, waiting for transfers between devices: 40.4 us -> none  [the longest x1 40.4 us: per_device(): lax.psum_scatter(gram_terms, 'dim', scatter_dimension=0, tiled=True)]
    all_to_all x2 -> x0, starting transfers between devices: 34.1 us -> none  [the longest x1 19.3 us: per_device(): lax.all_to_all(send_ids, 'docs', split_axis=0, concat_axis=0, tiled=True)]
    dot_general x3 -> x0, matrix products: 13.3 us -> none  [the longest x1 7.19 us: outer_panel(): lax.dot_general(own_rows, piece, (((1,), (1,)), ((), ())), preferred_elem...]
    gather x1 -> x0, local copies, waits for them, and re-layouts: 12.3 us -> none  [per_device(): jnp.take(sketches, slot_doc, axis=0)]
    scatter x2 -> x0, local copies, waits for them, and re-layouts: 4.9 us -> none  [the longest x1 2.45 us: per_device(): jnp.full((position_count,), -1, jnp.int32).at[slot].set(local_index)]
  transfers between devices with their start and end apart: 5 -> 0, of which waited for: 3 -> 0; matrix products, arithmetic and copies ran while one was open for 7% -> 0% of each run, Pallas kernels for 0% -> 0%
where the time goes in v1:
time: 114 us; the launch traced here: 113 us
  Pallas kernels  108 us (95%)
  local copies, waits for them, and re-layouts  4.23 us (4%)
    pallas_call x1, Pallas kernels, per_device(): pl.pallas_call(functools.partial(kernel, (ny, nz, nx, cl)), out_shape=(ja...  108 us
    unnamed x2, local copies, waits for them, and re-layouts  2.94 us

profile of v1, /device:TPU:1, one launch (start us, length us, event | category | flops | bytes accessed | tf_op | source)
XLA Modules:
  0.0 113.3 jit_solution(13864607333415050811)
XLA Ops:
  0.6 1.3 %broadcast_in_dim.2.ids_ref = s32[8,512]{1,0:T(8,128)} broadcast(s32[512]{0:T(512)} %param.4), dimensions={1} | broadcast | bytes 18432 | tf_op jit(solution)/shard_map/broadcast_in_dim | solution.py:368
  1.9 108.4 %shard_map.50 = (f32[8,4096]{1,0:T(8,128)}, f32[8,1024]{1,0:T(8,128)}) custom-call(bf16[512,1024]{1,0:T(8,128)(2,1)} %sk_ref.1, s32[8,512]{1,0:T(8,128)} %broadcast_in_dim.2.ids_ref, bf16[1024,1024]{1,0:T(8,128)(2,1)} %qu_ref.1), custom_call_target="tpu_custom_call" | custom-call | tf_op jit(solution)/shard_map/pallas_call | solution.py:373
  110.3 1.6 %copy.7 = f32[8,4096]{1,0:T(8,128)} copy(f32[8,4096]{1,0:T(8,128)} %get-tuple-element.4) | data formatting | bytes 262144
  111.9 1.4 %copy.8 = f32[8,1024]{1,0:T(8,128)} copy(f32[8,1024]{1,0:T(8,128)} %get-tuple-element.5) | data formatting | bytes 65536

commit v2 on v1

v2 whole, which is shorter than its diff:
```python
import functools
import math

import jax
import jax.numpy as jnp
from jax import lax
from jax.experimental import pallas as pl
from jax.experimental.pallas import tpu as pltpu
from jax.sharding import PartitionSpec as P

MESH = pl.DeviceIdType.MESH
CL = 64
NY = 4
LN2 = math.log(2.0)
BITS = 15


def power(level):
    return jnp.exp(level * LN2).astype(jnp.bfloat16).astype(jnp.float32)


def quantise(part):
    peak = jnp.maximum(jnp.max(jnp.abs(part), axis=0, keepdims=True), 1e-30)
    level = jnp.floor(jnp.log(peak) * (1.0 / LN2) + 0.001) + 1.0
    values = jnp.round(part * power(BITS - level)).astype(jnp.int32).astype(jnp.int16)
    levels = jnp.broadcast_to(level, (16, part.shape[1])).astype(jnp.int32).astype(jnp.int16)
    return values, levels


def restore(values, levels):
    level = levels.astype(jnp.int32).astype(jnp.float32)[0:1]
    return values.astype(jnp.int32).astype(jnp.float32) * power(level - BITS)


def kernel(
    sizes, sk_ref, ids_ref, qu_ref, gram_ref, scores_ref,
    docs_in, ids_in, quer, zpos, row, far, acc, rs_out, rs_in, own_cols, cols, rows,
    part, pair_in, half, x_in, done, packed, y_in, s_part, s_pair_in, s_half, s_x_in,
    local_sem, a_ss, a_rs, i_ss, i_rs, rs_ss, rs_rs, c_ss, c_rs, r_ss, r_rs, g_ss, g_rs,
    p_ss, p_rs, x_ss, x_rs, f_ss, f_rs, sp_ss, sp_rs, sx_ss, sx_rs,
):
    ny, nz, nx, cl = sizes
    n_docs, kd = sk_ref.shape
    members = 2 * ny
    kq = kd // members
    pairs = nz // 2
    n_rows = members * cl // 2
    hops = pairs // 2
    groups = pairs // 2
    dims = 2 * nx

    docs_at = lax.axis_index("docs")
    dim_at = lax.axis_index("dim")
    y, z = docs_at // nz, docs_at % nz
    zz, zp = z // 2, z % 2
    x, core = dim_at // 2, dim_at % 2

    def dev(yy, zz, zp, xx, cc):
        return (yy * nz + zz * 2 + zp, xx * 2 + cc)

    def member(o):
        return ((y + o // 2) % ny) * 2 + (zp + o % 2) % 2

    def member_from(o):
        return ((y + ny - o // 2) % ny) * 2 + (zp + o % 2) % 2

    def peer(o):
        return dev((y + o // 2) % ny, zz, (zp + o % 2) % 2, x, core)

    def x_peer(o):
        return dev(y, zz, zp, (x + o) % nx, core)

    z_next = (dev(y, (zz + 1) % pairs, zp, x, core), dev(y, (zz + pairs - 1) % pairs, zp, x, core))
    mate = dev(y, zz, zp, x, 1 - core)

    def remote(src, dst, ssem, rsem, to):
        return pltpu.make_async_remote_copy(
            src_ref=src, dst_ref=dst, send_sem=ssem, recv_sem=rsem, device_id=to, device_id_type=MESH
        )

    own_docs = pltpu.make_async_copy(
        sk_ref.at[:, pl.ds(pl.multiple_of(member(0) * kq, kq), kq)], docs_in.at[0], local_sem.at[0]
    )
    own_docs.start()

    barrier = pltpu.get_barrier_semaphore()
    partners = [peer(o) for o in range(1, members)] + [x_peer(o) for o in range(1, nx)] + list(z_next) + [mate]
    for to in partners:
        pl.semaphore_signal(barrier, inc=1, device_id=to, device_id_type=MESH)
    pl.semaphore_wait(barrier, len(partners))

    def ids_copy(o):
        return remote(ids_ref, ids_in.at[o], i_ss.at[o], i_rs.at[o], peer(o))

    def docs_copy(o):
        at = pl.multiple_of(member(o) * kq, kq)
        return remote(sk_ref.at[:, pl.ds(at, kq)], docs_in.at[o], a_ss.at[o], a_rs.at[o], peer(o))

    for o in range(1, members):
        ids_copy(o).start()
    for o in range(1, members):
        docs_copy(o).start()
    own_quer = pltpu.make_async_copy(qu_ref, quer, local_sem.at[1])
    own_quer.start()
    ids_in[0] = ids_ref[...]

    def place(o):
        ids = ids_in[o]
        owner = lax.shift_right_logical(ids, int(math.log2(cl)))
        local = lax.bitwise_and(ids, cl - 1)
        zpos[o] = lax.bitwise_and(lax.shift_right_logical(owner, 1), pairs - 1)
        who = lax.shift_right_logical(owner, int(math.log2(nz))) * 2 + lax.bitwise_and(owner, 1)
        upper = lax.shift_right_logical(local, int(math.log2(cl // 2)))
        row[o] = upper * n_rows + who * (cl // 2) + lax.bitwise_and(local, cl // 2 - 1)

    def onehot(o, target):
        places = lax.broadcasted_iota(jnp.int32, (2 * n_rows, n_docs), 0)
        here = jnp.where(zpos[o, 0:1, :] == target, row[o, 0:1, :], -1)
        return (here == places).astype(jnp.float32).astype(jnp.bfloat16)

    def sums(target):
        hot = jnp.concatenate([onehot(o, target) for o in range(members)], axis=1)
        return jnp.dot(hot, docs_in[...].reshape(members * n_docs, kq), preferred_element_type=jnp.float32)

    def rs_copy(way, h, s):
        return remote(
            rs_out.at[way, h, s], rs_in.at[way, h, s], rs_ss.at[way, h, s], rs_rs.at[way, h, s], z_next[way]
        )

    def rs_send(way, h, s, value):
        values, levels = quantise(value)
        rs_out[way, h, s, 0:n_rows] = values
        rs_out[way, h, s, n_rows : n_rows + 16] = levels
        rs_copy(way, h, s).start()

    def rs_got(way, h, s):
        rs_copy(way, h, s).wait_recv()
        return restore(rs_in[way, h, s, 0:n_rows], rs_in[way, h, s, n_rows : n_rows + 16])

    def mine(way, h):
        return acc[way, h * n_rows : (h + 1) * n_rows]

    first = [(zz + hops) % pairs, (zz + hops - 1) % pairs, (zz + pairs - hops + 1) % pairs]
    for o in range(members):
        if o:
            ids_copy(o).wait_recv()
            place(o)
            docs_copy(o).wait_recv()
        else:
            place(o)
            own_docs.wait()
        hot = jnp.concatenate([onehot(o, t) for t in first], axis=0)
        terms = jnp.dot(hot, docs_in[o], preferred_element_type=jnp.float32)
        for n, ref in enumerate((far, acc.at[0], acc.at[1])):
            term = terms[n * 2 * n_rows : (n + 1) * 2 * n_rows]
            ref[...] = term if o == 0 else ref[...] + term

    for s in range(hops):
        for h in range(2):
            for way in range(2):
                if s == 0:
                    if way == h:
                        rs_send(way, h, s, far[h * n_rows : (h + 1) * n_rows])
                elif s == 1 and way != h:
                    rs_send(way, h, s, mine(way, h))
                else:
                    rs_send(way, h, s, mine(way, h) + rs_got(way, h, s - 1))
        if s == 0:
            pass
        elif s + 1 < hops:
            acc[0] = sums((zz + hops - s - 1) % pairs)
            acc[1] = sums((zz + pairs - hops + s + 1) % pairs)
        else:
            acc[0] = sums(zz)

    def c_copy(h, o):
        return remote(own_cols.at[h, member(o)], cols.at[0, h, o], c_ss.at[h, o], c_rs.at[h, o], peer(o))

    def g_copy(way, h, d):
        if way == 0:
            src, dst = (pairs - d + 1) % pairs, pairs - d
        else:
            src, dst = d - 1, d
        return remote(
            cols.at[src, h], cols.at[dst, h], g_ss.at[way, h, d - 1], g_rs.at[way, h, d - 1], z_next[way]
        )

    own = []
    for h in range(2):
        own.append(mine(0, h) + rs_got(0, h, hops - 1) + rs_got(1, h, hops - 1))
        own_cols[h] = own[h].astype(jnp.bfloat16).reshape(members, cl // 2, kq)
        for o in range(1, members):
            c_copy(h, o).start()
        cols[0, h, 0] = own_cols[h, member(0)]
    order = [value.reshape(members, nx, 8, kq) for value in own]
    rows[0] = jnp.concatenate(
        [
            order[(2 * xx + cc) // nx][m, (2 * xx + cc) % nx]
            for cc in range(2) for xx in range(nx) for m in range(members)
        ],
        axis=0,
    ).astype(jnp.bfloat16)

    def r_copy(o):
        if o == 1:
            return remote(rows.at[0], rows.at[1], r_ss.at[1], r_rs.at[1], peer(1))
        return remote(rows.at[o % 2], rows.at[o], r_ss.at[o], r_rs.at[o], peer(o - o % 2))

    r_copy(1).start()
    for o in range(2, members, 2):
        r_copy(o).start()

    for h in range(2):
        for o in range(1, members):
            c_copy(h, o).wait_recv()
        for way in range(2):
            g_copy(way, h, 1).start()

    own_quer.wait()

    def wide(at):
        return jnp.concatenate(
            [jnp.concatenate([cols[at, h, o] for o in range(members)], axis=1) for h in range(2)], axis=0
        )

    asked = jnp.concatenate(
        [quer[:, pl.ds(pl.multiple_of(member_from(o) * kq, kq), kq)] for o in range(members)], axis=1
    )
    total = lax.dot_general(wide(0), asked, (((1,), (1,)), ((), ())), preferred_element_type=jnp.float32)
    total = total.reshape(nx, 2, 8, total.shape[1])
    for cc in range(2):
        for xx in range(nx):
            s_part[cc, xx] = total[xx, cc]

    def sp_copy():
        return remote(s_part.at[1 - core], s_pair_in, sp_ss.at[0], sp_rs.at[0], mate)

    def sx_copy(o):
        return remote(s_half.at[(x + o) % nx], s_x_in.at[o], sx_ss.at[o], sx_rs.at[o], x_peer(o))

    sp_copy().start()
    r_copy(1).wait_recv()
    for o in range(3, members, 2):
        r_copy(o).start()

    def block(g, low, high):
        these = jnp.concatenate([rows[o] for o in range(members)], axis=1)
        those = jnp.concatenate([wide(low), wide(high)], axis=0)
        total = lax.dot_general(these, those, (((1,), (1,)), ((), ())), preferred_element_type=jnp.float32)
        part[g] = total.reshape(2, nx, members, 8, 2 * cl)
        p_copy(g).start()

    def p_copy(g):
        return remote(part.at[g, 1 - core], pair_in.at[g], p_ss.at[g], p_rs.at[g], mate)

    def x_copy(g, o):
        return remote(half.at[g, (x + o) % nx], x_in.at[g, o], x_ss.at[g, o], x_rs.at[g, o], x_peer(o))

    def pair_sum(g):
        p_copy(g).wait_recv()
        half[g] = part[g, core] + pair_in[g]
        for o in range(1, nx):
            x_copy(g, o).start()

    def x_sum(g, low, high):
        total = half[g, x]
        for o in range(1, nx):
            x_copy(g, o).wait_recv()
            total = total + x_in[g, o]
        turned = pltpu.roll(total.reshape(members * 8, 2 * cl), cl, 1).reshape(total.shape)
        for m in range(members):
            done[m, (zz + low) % pairs] = total[m]
            done[m, (zz + high) % pairs] = turned[m]

    spots = [(pairs - d, d) for d in range(1, hops)] + [(0, hops)]
    for d in range(1, hops + 1):
        for h in range(2):
            for way in range(2):
                if d < hops or way == h:
                    g_copy(way, h, d).wait_recv()
                    if d + 1 < hops or (d + 1 == hops and way == h):
                        g_copy(way, h, d + 1).start()
        if d == 1:
            sp_copy().wait_recv()
            s_half[...] = s_part[core] + s_pair_in[...]
            for o in range(1, nx):
                sx_copy(o).start()
            for o in range(2, members):
                r_copy(o).wait_recv()
        block(d - 1, *spots[d - 1])
        if d >= 2:
            pair_sum(d - 2)
        if d >= 3:
            x_sum(d - 3, *spots[d - 3])
    total = s_half[x]
    for o in range(1, nx):
        sx_copy(o).wait_recv()
        total = total + s_x_in[o]
    scores_ref[...] = total * ((kd * dims) ** -0.5)
    if hops >= 2:
        x_sum(hops - 2, *spots[hops - 2])
    pair_sum(hops - 1)
    x_sum(hops - 1, *spots[hops - 1])

    lower = lax.broadcasted_iota(jnp.int32, (8, 2 * cl), 1) < cl
    for m in range(members):
        for t in range(pairs // 2):
            packed[m, t] = jnp.where(lower, done[m, 2 * t], pltpu.roll(done[m, 2 * t + 1], cl, 1))

    def f_copy(o):
        return remote(packed.at[member(o)], y_in.at[o], f_ss.at[o], f_rs.at[o], peer(o))

    for o in range(1, members):
        f_copy(o).start()
    y_in[0] = packed[member(0)]
    scale = 1.0 / (kd * dims)
    width = nz * cl
    for o in range(0, members, 2):
        for p in range(2):
            if o + p:
                f_copy(o + p).wait_recv()
        same, other = y_in[o], y_in[o + 1]
        even = jnp.where(zp == 0, same, other) * scale
        odd = jnp.where(zp == 0, other, same) * scale
        tiles = []
        for t in range(pairs // 2):
            tiles.append(jnp.where(lower, even[t], pltpu.roll(odd[t], cl, 1)))
            tiles.append(jnp.where(lower, pltpu.roll(even[t], cl, 1), odd[t]))
        at = pl.multiple_of(((y + ny - o // 2) % ny) * width, width)
        gram_ref[:, pl.ds(at, width)] = jnp.concatenate(tiles, axis=1)

    for o in range(1, members):
        ids_copy(o).wait_send()
        docs_copy(o).wait_send()
        for h in range(2):
            c_copy(h, o).wait_send()
        r_copy(o).wait_send()
        f_copy(o).wait_send()
    sp_copy().wait_send()
    for o in range(1, nx):
        sx_copy(o).wait_send()
    for s in range(hops):
        for way in range(2):
            for h in range(2):
                if s or way == h:
                    rs_copy(way, h, s).wait_send()
                if s + 1 < hops or way == h:
                    g_copy(way, h, s + 1).wait_send()
    for g in range(groups):
        p_copy(g).wait_send()
        for o in range(1, nx):
            x_copy(g, o).wait_send()


def per_device(ny, cl, sketches, clusters, queries):
    nz = lax.axis_size("docs") // ny
    nx = lax.axis_size("dim") // 2
    n_docs, kd = sketches.shape
    nq = queries.shape[0]
    members, pairs = 2 * ny, nz // 2
    kq, rows, hops, groups = kd // members, members * cl, pairs // 2, pairs // 2
    ids = clusters.reshape(1, n_docs)
    f32, bf16, i32, i16 = jnp.float32, jnp.bfloat16, jnp.int32, jnp.int16
    vmem, dma = pltpu.VMEM, pltpu.SemaphoreType.DMA
    whole = pl.BlockSpec(memory_space=pltpu.VMEM)
    away = pl.BlockSpec(memory_space=pl.ANY)
    return pl.pallas_call(
        functools.partial(kernel, (ny, nz, nx, cl)),
        out_shape=(
            jax.ShapeDtypeStruct((8, ny * nz * cl), f32),
            jax.ShapeDtypeStruct((8, nq), f32),
        ),
        in_specs=[away, whole, away],
        out_specs=(whole, whole),
        scratch_shapes=[
            vmem((members, n_docs, kq), bf16),
            vmem((members, 1, n_docs), i32),
            vmem((nq, kd), bf16),
            vmem((members, 1, n_docs), i32),
            vmem((members, 1, n_docs), i32),
            vmem((rows, kq), f32),
            vmem((2, rows, kq), f32),
            vmem((2, 2, hops, rows // 2 + 16, kq), i16),
            vmem((2, 2, hops, rows // 2 + 16, kq), i16),
            vmem((2, members, cl // 2, kq), bf16),
            vmem((pairs, 2, members, cl // 2, kq), bf16),
            vmem((members, rows, kq), bf16),
            vmem((groups, 2, nx, members, 8, 2 * cl), f32),
            vmem((groups, nx, members, 8, 2 * cl), f32),
            vmem((groups, nx, members, 8, 2 * cl), f32),
            vmem((groups, nx, members, 8, 2 * cl), f32),
            vmem((members, pairs, 8, 2 * cl), f32),
            vmem((members, pairs // 2, 8, 2 * cl), f32),
            vmem((members, pairs // 2, 8, 2 * cl), f32),
            vmem((2, nx, 8, nq), f32),
            vmem((nx, 8, nq), f32),
            vmem((nx, 8, nq), f32),
            vmem((nx, 8, nq), f32),
            dma((2,)),
            dma((members,)), dma((members,)),
            dma((members,)), dma((members,)),
            dma((2, 2, hops)), dma((2, 2, hops)),
            dma((2, members)), dma((2, members)),
            dma((members,)), dma((members,)),
            dma((2, 2, hops)), dma((2, 2, hops)),
            dma((groups,)), dma((groups,)),
            dma((groups, nx)), dma((groups, nx)),
            dma((members,)), dma((members,)),
            dma((1,)), dma((1,)),
            dma((nx,)), dma((nx,)),
        ],
        compiler_params=pltpu.CompilerParams(
            collective_id=0, has_side_effects=True, vmem_limit_bytes=56 * 1024 * 1024
        ),
    )(sketches, ids, queries)


def solution(mesh, ny=NY, cl=CL):
    in_specs = (P("docs", "dim"), P("docs"), P(None, "dim"))
    out_specs = (P(("docs", "dim"), None), P(("docs", "dim"), None))
    return jax.shard_map(
        functools.partial(per_device, ny, cl), mesh=mesh, in_specs=in_specs, out_specs=out_specs, check_vma=False
    )
```

time: 114 us -> 107 us (0.939)
  the two profiles are of different devices: /device:TPU:1 before, /device:TPU:32 now
where the time goes in v2:
time: 107 us
  Pallas kernels  103 us (96%)
  local copies, waits for them, and re-layouts  2.94 us (3%)
    pallas_call x1, Pallas kernels, per_device(): pl.pallas_call(functools.partial(kernel, (ny, nz, nx, cl)), out_shape=(ja...  103 us
    unnamed x2, local copies, waits for them, and re-layouts  2.94 us

profile of v2, /device:TPU:32, one launch (start us, length us, event | category | flops | bytes accessed | tf_op | source)
XLA Modules:
  0.0 106.9 jit_solution(3975539410087361925)
XLA Ops:
  0.6 103.3 %shard_map.50 = (f32[8,4096]{1,0:T(8,128)}, f32[8,1024]{1,0:T(8,128)}) custom-call(bf16[512,1024]{1,0:T(8,128)(2,1)} %sk_ref.1, s32[1,512]{1,0:T(1,128)} %bitcast.1, bf16[1024,1024]{1,0:T(8,128)(2,1)} %qu_ref.1), custom_call_target="tpu_custom_call" | custom-call | tf_op jit(solution)/shard_map/pallas_call | solution.py:367
  104.0 1.6 %copy.7 = f32[8,4096]{1,0:T(8,128)} copy(f32[8,4096]{1,0:T(8,128)} %get-tuple-element.4) | data formatting | bytes 262144
  105.5 1.4 %copy.8 = f32[8,1024]{1,0:T(8,128)} copy(f32[8,1024]{1,0:T(8,128)} %get-tuple-element.5) | data formatting | bytes 65536

commit v3 on v2

--- a/solution.py
+++ b/solution.py
@@ -35,7 +35,8 @@
 def kernel(
     sizes, sk_ref, ids_ref, qu_ref, gram_ref, scores_ref,
     docs_in, ids_in, quer, zpos, row, far, acc, rs_out, rs_in, own_cols, cols, rows,
-    part, pair_in, half, x_in, done, packed, y_in, s_part, s_pair_in, s_half, s_x_in,
+    part, pair_in, half, x_in, done, f_in, e_part, e_pair_in, e_half, e_x_in, e_done, e_f_in,
+    s_part, s_pair_in, s_half, s_x_in,
     local_sem, a_ss, a_rs, i_ss, i_rs, rs_ss, rs_rs, c_ss, c_rs, r_ss, r_rs, g_ss, g_rs,
     p_ss, p_rs, x_ss, x_rs, f_ss, f_rs, sp_ss, sp_rs, sx_ss, sx_rs,
 ):
@@ -46,7 +47,7 @@
     pairs = nz // 2
     n_rows = members * cl // 2
     hops = pairs // 2
-    groups = pairs // 2
+    last = hops - 1
     dims = 2 * nx
 
     docs_at = lax.axis_index("docs")
@@ -82,6 +83,8 @@
         sk_ref.at[:, pl.ds(pl.multiple_of(member(0) * kq, kq), kq)], docs_in.at[0], local_sem.at[0]
     )
     own_docs.start()
+    own_ids = pltpu.make_async_copy(ids_ref, ids_in.at[0], local_sem.at[2])
+    own_ids.start()
 
     barrier = pltpu.get_barrier_semaphore()
     partners = [peer(o) for o in range(1, members)] + [x_peer(o) for o in range(1, nx)] + list(z_next) + [mate]
@@ -102,7 +105,6 @@
         docs_copy(o).start()
     own_quer = pltpu.make_async_copy(qu_ref, quer, local_sem.at[1])
     own_quer.start()
-    ids_in[0] = ids_ref[...]
 
     def place(o):
         ids = ids_in[o]
@@ -141,33 +143,42 @@
         return acc[way, h * n_rows : (h + 1) * n_rows]
 
     first = [(zz + hops) % pairs, (zz + hops - 1) % pairs, (zz + pairs - hops + 1) % pairs]
-    for o in range(members):
+    def arrived(o):
         if o:
             ids_copy(o).wait_recv()
             place(o)
             docs_copy(o).wait_recv()
         else:
+            own_ids.wait()
             place(o)
             own_docs.wait()
+
+    near = sorted(range(members), key=lambda o: (min(o // 2, ny - o // 2), o % 2))
+    for o in near[:-1]:
+        arrived(o)
         hot = jnp.concatenate([onehot(o, t) for t in first], axis=0)
         terms = jnp.dot(hot, docs_in[o], preferred_element_type=jnp.float32)
         for n, ref in enumerate((far, acc.at[0], acc.at[1])):
             term = terms[n * 2 * n_rows : (n + 1) * 2 * n_rows]
-            ref[...] = term if o == 0 else ref[...] + term
-
-    for s in range(hops):
+            ref[...] = term if o == near[0] else ref[...] + term
+    o = near[-1]
+    arrived(o)
+    term = far[...] + jnp.dot(onehot(o, first[0]), docs_in[o], preferred_element_type=jnp.float32)
+    rs_send(0, 0, 0, term[:n_rows])
+    rs_send(1, 1, 0, term[n_rows:])
+    for n in range(2):
+        acc[n] += jnp.dot(onehot(o, first[n + 1]), docs_in[o], preferred_element_type=jnp.float32)
+
+    for s in range(1, hops):
         for h in range(2):
             for way in range(2):
-                if s == 0:
-                    if way == h:
-                        rs_send(way, h, s, far[h * n_rows : (h + 1) * n_rows])
-                elif s == 1 and way != h:
+                if s == 1 and way != h:
                     rs_send(way, h, s, mine(way, h))
-                else:
+        for h in range(2):
+            for way in range(2):
+                if s > 1 or way == h:
                     rs_send(way, h, s, mine(way, h) + rs_got(way, h, s - 1))
-        if s == 0:
-            pass
-        elif s + 1 < hops:
+        if s + 1 < hops:
             acc[0] = sums((zz + hops - s - 1) % pairs)
             acc[1] = sums((zz + pairs - hops + s + 1) % pairs)
         else:
@@ -176,13 +187,17 @@
     def c_copy(h, o):
         return remote(own_cols.at[h, member(o)], cols.at[0, h, o], c_ss.at[h, o], c_rs.at[h, o], peer(o))
 
-    def g_copy(way, h, d):
+    quarter = members // 2
+
+    def g_copy(way, e, d):
         if way == 0:
             src, dst = (pairs - d + 1) % pairs, pairs - d
         else:
             src, dst = d - 1, d
+        h, those = e // 2, pl.ds(e % 2 * quarter, quarter)
         return remote(
-            cols.at[src, h], cols.at[dst, h], g_ss.at[way, h, d - 1], g_rs.at[way, h, d - 1], z_next[way]
+            cols.at[src, h, those], cols.at[dst, h, those],
+            g_ss.at[way, e, d - 1], g_rs.at[way, e, d - 1], z_next[way],
         )
 
     own = []
@@ -210,11 +225,21 @@
     for o in range(2, members, 2):
         r_copy(o).start()
 
-    for h in range(2):
-        for o in range(1, members):
-            c_copy(h, o).wait_recv()
+    for e in range(4):
+        for o in range(max(1, e % 2 * quarter), (e % 2 + 1) * quarter):
+            c_copy(e // 2, o).wait_recv()
         for way in range(2):
-            g_copy(way, h, 1).start()
+            g_copy(way, e, 1).start()
+
+    def sp_copy():
+        return remote(s_part.at[1 - core], s_pair_in, sp_ss.at[0], sp_rs.at[0], mate)
+
+    def sx_copy(o):
+        return remote(s_half.at[(x + o) % nx], s_x_in.at[o], sx_ss.at[o], sx_rs.at[o], x_peer(o))
+
+    r_copy(1).wait_recv()
+    for o in range(3, members, 2):
+        r_copy(o).start()
 
     own_quer.wait()
 
@@ -231,103 +256,134 @@
     for cc in range(2):
         for xx in range(nx):
             s_part[cc, xx] = total[xx, cc]
-
-    def sp_copy():
-        return remote(s_part.at[1 - core], s_pair_in, sp_ss.at[0], sp_rs.at[0], mate)
-
-    def sx_copy(o):
-        return remote(s_half.at[(x + o) % nx], s_x_in.at[o], sx_ss.at[o], sx_rs.at[o], x_peer(o))
-
     sp_copy().start()
-    r_copy(1).wait_recv()
-    for o in range(3, members, 2):
-        r_copy(o).start()
-
-    def block(g, low, high):
+
+    lower = lax.broadcasted_iota(jnp.int32, (8, 2 * cl), 1) < cl
+
+    def turn(tile):
+        return pltpu.roll(tile, cl, 1)
+
+    def p_copy(g):
+        src, dst = (part.at[g], pair_in.at[g]) if g < last else (e_part.at[g - last], e_pair_in.at[g - last])
+        return remote(src.at[1 - core], dst, p_ss.at[g], p_rs.at[g], mate)
+
+    def x_copy(g, o):
+        src, dst = (half.at[g], x_in.at[g]) if g < last else (e_half.at[g - last], e_x_in.at[g - last])
+        return remote(src.at[(x + o) % nx], dst.at[o], x_ss.at[g, o], x_rs.at[g, o], x_peer(o))
+
+    def f_copy(g, o):
+        if g < last:
+            src, dst = done.at[g, member(o)], f_in.at[g, o]
+        else:
+            src, dst = e_done.at[g - last, member(o) // 2], e_f_in.at[g - last, o]
+        return remote(src, dst, f_ss.at[g, o], f_rs.at[g, o], peer(o))
+
+    def block(g):
         these = jnp.concatenate([rows[o] for o in range(members)], axis=1)
-        those = jnp.concatenate([wide(low), wide(high)], axis=0)
+        if g < last:
+            those = jnp.concatenate([wide(pairs - g - 1), wide(g + 1)], axis=0)
+        else:
+            those = jnp.concatenate([wide((g - last) * hops)] * 2, axis=0)
         total = lax.dot_general(these, those, (((1,), (1,)), ((), ())), preferred_element_type=jnp.float32)
-        part[g] = total.reshape(2, nx, members, 8, 2 * cl)
+        total = total.reshape(2, nx, members, 8, 2 * cl)
+        if g < last:
+            part[g] = total
+        else:
+            two = total.reshape(2, nx, members // 2, 2, 8, 2 * cl)
+            e_part[g - last] = jnp.where(lower, two[:, :, :, 0], two[:, :, :, 1])
         p_copy(g).start()
-
-    def p_copy(g):
-        return remote(part.at[g, 1 - core], pair_in.at[g], p_ss.at[g], p_rs.at[g], mate)
-
-    def x_copy(g, o):
-        return remote(half.at[g, (x + o) % nx], x_in.at[g, o], x_ss.at[g, o], x_rs.at[g, o], x_peer(o))
 
     def pair_sum(g):
         p_copy(g).wait_recv()
-        half[g] = part[g, core] + pair_in[g]
+        if g < last:
+            half[g] = part[g, core] + pair_in[g]
+        else:
+            e_half[g - last] = e_part[g - last, core] + e_pair_in[g - last]
         for o in range(1, nx):
             x_copy(g, o).start()
 
-    def x_sum(g, low, high):
-        total = half[g, x]
+    def x_sum(g):
+        mine, other = (half.at[g], x_in.at[g]) if g < last else (e_half.at[g - last], e_x_in.at[g - last])
+        total = mine[x]
         for o in range(1, nx):
             x_copy(g, o).wait_recv()
-            total = total + x_in[g, o]
-        turned = pltpu.roll(total.reshape(members * 8, 2 * cl), cl, 1).reshape(total.shape)
-        for m in range(members):
-            done[m, (zz + low) % pairs] = total[m]
-            done[m, (zz + high) % pairs] = turned[m]
-
-    spots = [(pairs - d, d) for d in range(1, hops)] + [(0, hops)]
+            total = total + other[o]
+        if g < last:
+            done[g] = total
+            f_in[g, 0] = done[g, member(0)]
+        else:
+            e_done[g - last] = total
+            e_f_in[g - last, 0] = e_done[g - last, member(0) // 2]
+        for o in range(1, members):
+            f_copy(g, o).start()
+
+    scale = 1.0 / (kd * dims)
+
+    def store(at, tile):
+        gram_ref[:, pl.ds(pl.multiple_of(at * 2 * cl, 2 * cl), 2 * cl)] = tile
+
+    def finish(g):
+        for o in range(1, members):
+            f_copy(g, o).wait_recv()
+        for o in range(0, members, 2):
+            at = ((y + ny - o // 2) % ny) * pairs
+            same, other = (f_in[g, o], f_in[g, o + 1]) if g < last else (e_f_in[g - last, o], e_f_in[g - last, o + 1])
+            even = jnp.where(zp == 0, same, other) * scale
+            odd = jnp.where(zp == 0, other, same) * scale
+            left = jnp.where(lower, even, turn(odd))
+            right = jnp.where(lower, turn(even), odd)
+            if g < last:
+                store(at + (zz + pairs - g - 1) % pairs, left)
+                store(at + (zz + g + 1) % pairs, right)
+            else:
+                store(at + (zz + (g - last) * hops) % pairs, jnp.where(zp == 0, left, right))
+
+    before, waiting = [], []
     for d in range(1, hops + 1):
-        for h in range(2):
+        for e in range(4):
             for way in range(2):
-                if d < hops or way == h:
-                    g_copy(way, h, d).wait_recv()
-                    if d + 1 < hops or (d + 1 == hops and way == h):
-                        g_copy(way, h, d + 1).start()
+                if d < hops or way == e // 2:
+                    g_copy(way, e, d).wait_recv()
+                    if d + 1 < hops or (d + 1 == hops and way == e // 2):
+                        g_copy(way, e, d + 1).start()
         if d == 1:
             sp_copy().wait_recv()
             s_half[...] = s_part[core] + s_pair_in[...]
             for o in range(1, nx):
                 sx_copy(o).start()
+        if d == min(2, last):
             for o in range(2, members):
                 r_copy(o).wait_recv()
-        block(d - 1, *spots[d - 1])
-        if d >= 2:
-            pair_sum(d - 2)
-        if d >= 3:
-            x_sum(d - 3, *spots[d - 3])
+            now = [last]
+        else:
+            now = []
+        if 2 <= d < hops:
+            now.append(d - 2)
+        if d == last:
+            now.append(last - 1)
+        if d < hops:
+            for g in waiting:
+                pair_sum(g)
+            for g in now:
+                block(g)
+            before, waiting = before + waiting, now
+        if d == last:
+            for g in waiting:
+                pair_sum(g)
+    block(hops)
+    before = before + waiting
+    for g in before[:-1]:
+        x_sum(g)
+    pair_sum(hops)
+    x_sum(before[-1])
     total = s_half[x]
     for o in range(1, nx):
         sx_copy(o).wait_recv()
         total = total + s_x_in[o]
     scores_ref[...] = total * ((kd * dims) ** -0.5)
-    if hops >= 2:
-        x_sum(hops - 2, *spots[hops - 2])
-    pair_sum(hops - 1)
-    x_sum(hops - 1, *spots[hops - 1])
-
-    lower = lax.broadcasted_iota(jnp.int32, (8, 2 * cl), 1) < cl
-    for m in range(members):
-        for t in range(pairs // 2):
-            packed[m, t] = jnp.where(lower, done[m, 2 * t], pltpu.roll(done[m, 2 * t + 1], cl, 1))
-
-    def f_copy(o):
-        return remote(packed.at[member(o)], y_in.at[o], f_ss.at[o], f_rs.at[o], peer(o))
-
-    for o in range(1, members):
-        f_copy(o).start()
-    y_in[0] = packed[member(0)]
-    scale = 1.0 / (kd * dims)
-    width = nz * cl
-    for o in range(0, members, 2):
-        for p in range(2):
-            if o + p:
-                f_copy(o + p).wait_recv()
-        same, other = y_in[o], y_in[o + 1]
-        even = jnp.where(zp == 0, same, other) * scale
-        odd = jnp.where(zp == 0, other, same) * scale
-        tiles = []
-        for t in range(pairs // 2):
-            tiles.append(jnp.where(lower, even[t], pltpu.roll(odd[t], cl, 1)))
-            tiles.append(jnp.where(lower, pltpu.roll(even[t], cl, 1), odd[t]))
-        at = pl.multiple_of(((y + ny - o // 2) % ny) * width, width)
-        gram_ref[:, pl.ds(at, width)] = jnp.concatenate(tiles, axis=1)
+    x_sum(hops)
+    for g in before + [hops]:
+        finish(g)
 
     for o in range(1, members):
         ids_copy(o).wait_send()
@@ -335,21 +391,27 @@
         for h in range(2):
             c_copy(h, o).wait_send()
         r_copy(o).wait_send()
-        f_copy(o).wait_send()
     sp_copy().wait_send()
     for o in range(1, nx):
         sx_copy(o).wait_send()
     for s in range(hops):
         for way in range(2):
-            for h in range(2):
-                if s or way == h:
-                    rs_copy(way, h, s).wait_send()
-                if s + 1 < hops or way == h:
-                    g_copy(way, h, s + 1).wait_send()
-    for g in range(groups):
+            for e in range(4):
+                if e < 2 and (s or way == e):
+                    rs_copy(way, e, s).wait_send()
+                if s + 1 < hops or way == e // 2:
+                    g_copy(way, e, s + 1).wait_send()
+    for g in range(hops + 1):
         p_copy(g).wait_send()
         for o in range(1, nx):
             x_copy(g, o).wait_send()
+        for o in range(1, members):
+            f_copy(g, o).wait_send()
+
+
+def hand_over(gram_in, scores_in, gram_ref, scores_ref):
+    gram_ref[...] = gram_in[...]
+    scores_ref[...] = scores_in[...]
 
 
 def per_device(ny, cl, sketches, clusters, queries):
@@ -358,19 +420,20 @@
     n_docs, kd = sketches.shape
     nq = queries.shape[0]
     members, pairs = 2 * ny, nz // 2
-    kq, rows, hops, groups = kd // members, members * cl, pairs // 2, pairs // 2
+    kq, rows, hops = kd // members, members * cl, pairs // 2
+    last = hops - 1
     ids = clusters.reshape(1, n_docs)
     f32, bf16, i32, i16 = jnp.float32, jnp.bfloat16, jnp.int32, jnp.int16
     vmem, dma = pltpu.VMEM, pltpu.SemaphoreType.DMA
     whole = pl.BlockSpec(memory_space=pltpu.VMEM)
     away = pl.BlockSpec(memory_space=pl.ANY)
-    return pl.pallas_call(
+    gram, scores = pl.pallas_call(
         functools.partial(kernel, (ny, nz, nx, cl)),
         out_shape=(
             jax.ShapeDtypeStruct((8, ny * nz * cl), f32),
             jax.ShapeDtypeStruct((8, nq), f32),
         ),
-        in_specs=[away, whole, away],
+        in_specs=[away, away, away],
         out_specs=(whole, whole),
         scratch_shapes=[
             vmem((members, n_docs, kq), bf16),
@@ -385,27 +448,32 @@
             vmem((2, members, cl // 2, kq), bf16),
             vmem((pairs, 2, members, cl // 2, kq), bf16),
             vmem((members, rows, kq), bf16),
-            vmem((groups, 2, nx, members, 8, 2 * cl), f32),
-            vmem((groups, nx, members, 8, 2 * cl), f32),
-            vmem((groups, nx, members, 8, 2 * cl), f32),
-            vmem((groups, nx, members, 8, 2 * cl), f32),
-            vmem((members, pairs, 8, 2 * cl), f32),
-            vmem((members, pairs // 2, 8, 2 * cl), f32),
-            vmem((members, pairs // 2, 8, 2 * cl), f32),
+            vmem((last, 2, nx, members, 8, 2 * cl), f32),
+            vmem((last, nx, members, 8, 2 * cl), f32),
+            vmem((last, nx, members, 8, 2 * cl), f32),
+            vmem((last, nx, members, 8, 2 * cl), f32),
+            vmem((last, members, 8, 2 * cl), f32),
+            vmem((last, members, 8, 2 * cl), f32),
+            vmem((2, 2, nx, members // 2, 8, 2 * cl), f32),
+            vmem((2, nx, members // 2, 8, 2 * cl), f32),
+            vmem((2, nx, members // 2, 8, 2 * cl), f32),
+            vmem((2, nx, members // 2, 8, 2 * cl), f32),
+            vmem((2, members // 2, 8, 2 * cl), f32),
+            vmem((2, members, 8, 2 * cl), f32),
             vmem((2, nx, 8, nq), f32),
             vmem((nx, 8, nq), f32),
             vmem((nx, 8, nq), f32),
             vmem((nx, 8, nq), f32),
-            dma((2,)),
+            dma((3,)),
             dma((members,)), dma((members,)),
             dma((members,)), dma((members,)),
             dma((2, 2, hops)), dma((2, 2, hops)),
             dma((2, members)), dma((2, members)),
             dma((members,)), dma((members,)),
-            dma((2, 2, hops)), dma((2, 2, hops)),
-            dma((groups,)), dma((groups,)),
-            dma((groups, nx)), dma((groups, nx)),
-            dma((members,)), dma((members,)),
+            dma((2, 4, hops)), dma((2, 4, hops)),
+            dma((hops + 1,)), dma((hops + 1,)),
+            dma((hops + 1, nx)), dma((hops + 1, nx)),
+            dma((hops + 1, members)), dma((hops + 1, members)),
             dma((1,)), dma((1,)),
             dma((nx,)), dma((nx,)),
         ],
@@ -413,6 +481,15 @@
             collective_id=0, has_side_effects=True, vmem_limit_bytes=56 * 1024 * 1024
         ),
     )(sketches, ids, queries)
+    return pl.pallas_call(
+        hand_over,
+        out_shape=(
+            jax.ShapeDtypeStruct((8, ny * nz * cl), f32),
+            jax.ShapeDtypeStruct((8, nq), f32),
+        ),
+        in_specs=[whole, whole],
+        out_specs=(whole, whole),
+    )(gram, scores)
 
 
 def solution(mesh, ny=NY, cl=CL):

time: 107 us -> 101 us (0.944)
  the two profiles are of different devices: /device:TPU:32 before, /device:TPU:1 now
where the time goes in v3:
time: 101 us; the launch traced here: 100 us
  Pallas kernels  99.8 us (99%)
    pallas_call x1, Pallas kernels, per_device(): pl.pallas_call(functools.partial(kernel, (ny, nz, nx, cl)), out_shape=(ja...  98.2 us

profile of v3, /device:TPU:1, one launch (start us, length us, event | category | flops | bytes accessed | tf_op | source)
XLA Modules:
  0.0 100.5 jit_solution(109092156145599660)
XLA Ops:
  0.6 98.2 %shard_map.50 = (f32[8,4096]{1,0:T(8,128)}, f32[8,1024]{1,0:T(8,128)}) custom-call(bf16[512,1024]{1,0:T(8,128)(2,1)} %sk_ref.1, s32[1,512]{1,0:T(1,128)} %bitcast.1, bf16[1024,1024]{1,0:T(8,128)(2,1)} %qu_ref.1), custom_call_target="tpu_custom_call" | custom-call | tf_op jit(solution)/shard_map/pallas_call | solution.py:430
  98.9 1.6 %shard_map.51 = (f32[8,4096]{1,0:T(8,128)}, f32[8,1024]{1,0:T(8,128)}) custom-call(f32[8,4096]{1,0:T(8,128)} %get-tuple-element.4.gram_in, f32[8,1024]{1,0:T(8,128)} %get-tuple-element.5.scores_in), custom_call_target="tpu_custom_call" | custom-call | tf_op jit(solution)/shard_map/pallas_call | solution.py:484

commit v4 on v3

--- a/solution.py
+++ b/solution.py
@@ -13,23 +13,35 @@
 NY = 4
 LN2 = math.log(2.0)
 BITS = 15
+FINE = 16
 
 
 def power(level):
     return jnp.exp(level * LN2).astype(jnp.bfloat16).astype(jnp.float32)
 
 
-def quantise(part):
-    peak = jnp.maximum(jnp.max(jnp.abs(part), axis=0, keepdims=True), 1e-30)
-    level = jnp.floor(jnp.log(peak) * (1.0 / LN2) + 0.001) + 1.0
-    values = jnp.round(part * power(BITS - level)).astype(jnp.int32).astype(jnp.int16)
-    levels = jnp.broadcast_to(level, (16, part.shape[1])).astype(jnp.int32).astype(jnp.int16)
-    return values, levels
-
-
-def restore(values, levels):
-    level = levels.astype(jnp.int32).astype(jnp.float32)[0:1]
-    return values.astype(jnp.int32).astype(jnp.float32) * power(level - BITS)
+def peak(part):
+    return jnp.maximum(jnp.max(jnp.abs(part), axis=0, keepdims=True), 1e-30)
+
+
+def code(bound):
+    return jnp.ceil(jnp.log(bound) * (FINE / LN2) + 0.01)
+
+
+def bound_of(fine):
+    return jnp.exp(fine * (LN2 / FINE))
+
+
+def level_of(fine):
+    return jnp.floor(fine * (1.0 / FINE)) + 1.0
+
+
+def quantise(part, fine):
+    return jnp.round(part * power(BITS - level_of(fine))).astype(jnp.int32).astype(jnp.int16)
+
+
+def restore(values, fine):
+    return values.astype(jnp.int32).astype(jnp.float32) * power(level_of(fine) - BITS)
 
 
 def kernel(
@@ -79,6 +91,12 @@
             src_ref=src, dst_ref=dst, send_sem=ssem, recv_sem=rsem, device_id=to, device_id_type=MESH
         )
 
+    def all_sent(ref, sem):
+        remote(ref, ref, sem, local_sem.at[0], mate).wait_send()
+
+    def all_got(ref, sem):
+        remote(ref, ref, local_sem.at[0], sem, mate).wait_recv()
+
     own_docs = pltpu.make_async_copy(
         sk_ref.at[:, pl.ds(pl.multiple_of(member(0) * kq, kq), kq)], docs_in.at[0], local_sem.at[0]
     )
@@ -93,11 +111,11 @@
     pl.semaphore_wait(barrier, len(partners))
 
     def ids_copy(o):
-        return remote(ids_ref, ids_in.at[o], i_ss.at[o], i_rs.at[o], peer(o))
+        return remote(ids_ref, ids_in.at[o], i_ss.at[0], i_rs.at[0], peer(o))
 
     def docs_copy(o):
         at = pl.multiple_of(member(o) * kq, kq)
-        return remote(sk_ref.at[:, pl.ds(at, kq)], docs_in.at[o], a_ss.at[o], a_rs.at[o], peer(o))
+        return remote(sk_ref.at[:, pl.ds(at, kq)], docs_in.at[o], a_ss.at[0], a_rs.at[o], peer(o))
 
     for o in range(1, members):
         ids_copy(o).start()
@@ -124,33 +142,50 @@
         hot = jnp.concatenate([onehot(o, target) for o in range(members)], axis=1)
         return jnp.dot(hot, docs_in[...].reshape(members * n_docs, kq), preferred_element_type=jnp.float32)
 
-    def rs_copy(way, h, s):
+    bit = n_rows // 2
+    spans = (pl.ds(0, bit + 16), pl.ds(bit + 16, bit))
+
+    def rs_copy(way, h, p, s):
         return remote(
-            rs_out.at[way, h, s], rs_in.at[way, h, s], rs_ss.at[way, h, s], rs_rs.at[way, h, s], z_next[way]
+            rs_out.at[way, h, s, spans[p]], rs_in.at[way, h, s, spans[p]],
+            rs_ss.at[way, h], rs_rs.at[way, h, p, s], z_next[way],
         )
 
+    def rs_start(way, h, p, s, value, fine):
+        values = quantise(value, fine)
+        if p == 0:
+            rs_out[way, h, s, 0:16] = jnp.broadcast_to(fine, (16, kq)).astype(jnp.int32).astype(jnp.int16)
+            rs_out[way, h, s, 16 : bit + 16] = values
+        else:
+            rs_out[way, h, s, bit + 16 : 2 * bit + 16] = values
+        rs_copy(way, h, p, s).start()
+
     def rs_send(way, h, s, value):
-        values, levels = quantise(value)
-        rs_out[way, h, s, 0:n_rows] = values
-        rs_out[way, h, s, n_rows : n_rows + 16] = levels
-        rs_copy(way, h, s).start()
-
-    def rs_got(way, h, s):
-        rs_copy(way, h, s).wait_recv()
-        return restore(rs_in[way, h, s, 0:n_rows], rs_in[way, h, s, n_rows : n_rows + 16])
+        fine = code(peak(value))
+        for p in range(2):
+            rs_start(way, h, p, s, value[p * bit : (p + 1) * bit], fine)
+
+    def rs_fine(way, h, s):
+        return rs_in[way, h, s, 0:16].astype(jnp.int32).astype(jnp.float32)[0:1]
+
+    def rs_got(way, h, p, s, fine):
+        at = 16 + p * bit
+        return restore(rs_in[way, h, s, at : at + bit], fine)
 
     def mine(way, h):
         return acc[way, h * n_rows : (h + 1) * n_rows]
 
     first = [(zz + hops) % pairs, (zz + hops - 1) % pairs, (zz + pairs - hops + 1) % pairs]
+    others = pl.ds(1, members - 1)
+    own_ids.wait()
+    all_got(ids_in.at[others], i_rs.at[0])
+    for o in range(members):
+        place(o)
+
     def arrived(o):
         if o:
-            ids_copy(o).wait_recv()
-            place(o)
             docs_copy(o).wait_recv()
         else:
-            own_ids.wait()
-            place(o)
             own_docs.wait()
 
     near = sorted(range(members), key=lambda o: (min(o // 2, ny - o // 2), o % 2))
@@ -174,20 +209,29 @@
             for way in range(2):
                 if s == 1 and way != h:
                     rs_send(way, h, s, mine(way, h))
+        chains = [(way, h) for h in range(2) for way in range(2) if s > 1 or way == h]
+        tops = {(way, h): peak(mine(way, h)) for way, h in chains}
+        fines = {}
         for h in range(2):
-            for way in range(2):
-                if s > 1 or way == h:
-                    rs_send(way, h, s, mine(way, h) + rs_got(way, h, s - 1))
+            for p in range(2):
+                for way in range(2):
+                    if (way, h) in tops:
+                        rs_copy(way, h, p, s - 1).wait_recv()
+                        before = rs_fine(way, h, s - 1)
+                        if p == 0:
+                            fines[way, h] = code(tops[way, h] + bound_of(before))
+                        value = mine(way, h)[p * bit : (p + 1) * bit] + rs_got(way, h, p, s - 1, before)
+                        rs_start(way, h, p, s, value, fines[way, h])
         if s + 1 < hops:
             acc[0] = sums((zz + hops - s - 1) % pairs)
             acc[1] = sums((zz + pairs - hops + s + 1) % pairs)
         else:
             acc[0] = sums(zz)
 
+    quarter = members // 2
+
     def c_copy(h, o):
-        return remote(own_cols.at[h, member(o)], cols.at[0, h, o], c_ss.at[h, o], c_rs.at[h, o], peer(o))
-
-    quarter = members // 2
+        return remote(own_cols.at[h, member(o)], cols.at[0, h, o], c_ss.at[0], c_rs.at[h, o // quarter], peer(o))
 
     def g_copy(way, e, d):
         if way == 0:
@@ -197,12 +241,19 @@
         h, those = e // 2, pl.ds(e % 2 * quarter, quarter)
         return remote(
             cols.at[src, h, those], cols.at[dst, h, those],
-            g_ss.at[way, e, d - 1], g_rs.at[way, e, d - 1], z_next[way],
+            g_ss.at[way, h], g_rs.at[way, e, d - 1], z_next[way],
         )
 
     own = []
     for h in range(2):
-        own.append(mine(0, h) + rs_got(0, h, hops - 1) + rs_got(1, h, hops - 1))
+        halves = []
+        for p in range(2):
+            value = mine(0, h)[p * bit : (p + 1) * bit]
+            for way in range(2):
+                rs_copy(way, h, p, hops - 1).wait_recv()
+                value = value + rs_got(way, h, p, hops - 1, rs_fine(way, h, hops - 1))
+            halves.append(value)
+        own.append(jnp.concatenate(halves, axis=0))
         own_cols[h] = own[h].astype(jnp.bfloat16).reshape(members, cl // 2, kq)
         for o in range(1, members):
             c_copy(h, o).start()
@@ -218,16 +269,16 @@
 
     def r_copy(o):
         if o == 1:
-            return remote(rows.at[0], rows.at[1], r_ss.at[1], r_rs.at[1], peer(1))
-        return remote(rows.at[o % 2], rows.at[o], r_ss.at[o], r_rs.at[o], peer(o - o % 2))
+            return remote(rows.at[0], rows.at[1], r_ss.at[0], r_rs.at[0], peer(1))
+        return remote(rows.at[o % 2], rows.at[o], r_ss.at[0], r_rs.at[1], peer(o - o % 2))
 
     r_copy(1).start()
     for o in range(2, members, 2):
         r_copy(o).start()
 
     for e in range(4):
-        for o in range(max(1, e % 2 * quarter), (e % 2 + 1) * quarter):
-            c_copy(e // 2, o).wait_recv()
+        begin = max(1, e % 2 * quarter)
+        all_got(cols.at[0, e // 2, pl.ds(begin, (e % 2 + 1) * quarter - begin)], c_rs.at[e // 2, e % 2])
         for way in range(2):
             g_copy(way, e, 1).start()
 
@@ -235,7 +286,7 @@
         return remote(s_part.at[1 - core], s_pair_in, sp_ss.at[0], sp_rs.at[0], mate)
 
     def sx_copy(o):
-        return remote(s_half.at[(x + o) % nx], s_x_in.at[o], sx_ss.at[o], sx_rs.at[o], x_peer(o))
+        return remote(s_half.at[(x + o) % nx], s_x_in.at[o], sx_ss.at[0], sx_rs.at[0], x_peer(o))
 
     r_copy(1).wait_recv()
     for o in range(3, members, 2):
@@ -258,6 +309,7 @@
             s_part[cc, xx] = total[xx, cc]
     sp_copy().start()
 
+    far_x = pl.ds(1, nx - 1)
     lower = lax.broadcasted_iota(jnp.int32, (8, 2 * cl), 1) < cl
 
     def turn(tile):
@@ -265,18 +317,18 @@
 
     def p_copy(g):
         src, dst = (part.at[g], pair_in.at[g]) if g < last else (e_part.at[g - last], e_pair_in.at[g - last])
-        return remote(src.at[1 - core], dst, p_ss.at[g], p_rs.at[g], mate)
+        return remote(src.at[1 - core], dst, p_ss.at[g // last], p_rs.at[g], mate)
 
     def x_copy(g, o):
         src, dst = (half.at[g], x_in.at[g]) if g < last else (e_half.at[g - last], e_x_in.at[g - last])
-        return remote(src.at[(x + o) % nx], dst.at[o], x_ss.at[g, o], x_rs.at[g, o], x_peer(o))
+        return remote(src.at[(x + o) % nx], dst.at[o], x_ss.at[g // last], x_rs.at[g], x_peer(o))
 
     def f_copy(g, o):
         if g < last:
             src, dst = done.at[g, member(o)], f_in.at[g, o]
         else:
             src, dst = e_done.at[g - last, member(o) // 2], e_f_in.at[g - last, o]
-        return remote(src, dst, f_ss.at[g, o], f_rs.at[g, o], peer(o))
+        return remote(src, dst, f_ss.at[g // last], f_rs.at[g], peer(o))
 
     def block(g):
         these = jnp.concatenate([rows[o] for o in range(members)], axis=1)
@@ -305,8 +357,8 @@
     def x_sum(g):
         mine, other = (half.at[g], x_in.at[g]) if g < last else (e_half.at[g - last], e_x_in.at[g - last])
         total = mine[x]
+        all_got(other.at[far_x], x_rs.at[g])
         for o in range(1, nx):
-            x_copy(g, o).wait_recv()
             total = total + other[o]
         if g < last:
             done[g] = total
@@ -323,8 +375,7 @@
         gram_ref[:, pl.ds(pl.multiple_of(at * 2 * cl, 2 * cl), 2 * cl)] = tile
 
     def finish(g):
-        for o in range(1, members):
-            f_copy(g, o).wait_recv()
+        all_got((f_in.at[g] if g < last else e_f_in.at[g - last]).at[others], f_rs.at[g])
         for o in range(0, members, 2):
             at = ((y + ny - o // 2) % ny) * pairs
             same, other = (f_in[g, o], f_in[g, o + 1]) if g < last else (e_f_in[g - last, o], e_f_in[g - last, o + 1])
@@ -347,13 +398,19 @@
                     if d + 1 < hops or (d + 1 == hops and way == e // 2):
                         g_copy(way, e, d + 1).start()
         if d == 1:
+            all_sent(ids_in.at[others], i_ss.at[0])
+            all_sent(docs_in.at[others], a_ss.at[0])
+            all_sent(cols.at[0, :, others], c_ss.at[0])
+            for way in range(2):
+                for h in range(2):
+                    begin = 0 if way == h else 1
+                    all_sent(rs_out.at[way, h, pl.ds(begin, hops - begin)], rs_ss.at[way, h])
             sp_copy().wait_recv()
             s_half[...] = s_part[core] + s_pair_in[...]
             for o in range(1, nx):
                 sx_copy(o).start()
         if d == min(2, last):
-            for o in range(2, members):
-                r_copy(o).wait_recv()
+            all_got(rows.at[pl.ds(2, members - 2)], r_rs.at[1])
             now = [last]
         else:
             now = []
@@ -377,36 +434,26 @@
     pair_sum(hops)
     x_sum(before[-1])
     total = s_half[x]
+    all_got(s_x_in.at[far_x], sx_rs.at[0])
     for o in range(1, nx):
-        sx_copy(o).wait_recv()
         total = total + s_x_in[o]
     scores_ref[...] = total * ((kd * dims) ** -0.5)
+    all_sent(rows.at[others], r_ss.at[0])
+    for way in range(2):
+        for h in range(2):
+            all_sent(cols.at[pl.ds(0, hops if way == h else hops - 1), h], g_ss.at[way, h])
+    sp_copy().wait_send()
+    all_sent(s_x_in.at[far_x], sx_ss.at[0])
+    all_sent(pair_in, p_ss.at[0])
+    all_sent(x_in.at[:, far_x], x_ss.at[0])
     x_sum(hops)
-    for g in before + [hops]:
+    for g in before:
         finish(g)
-
-    for o in range(1, members):
-        ids_copy(o).wait_send()
-        docs_copy(o).wait_send()
-        for h in range(2):
-            c_copy(h, o).wait_send()
-        r_copy(o).wait_send()
-    sp_copy().wait_send()
-    for o in range(1, nx):
-        sx_copy(o).wait_send()
-    for s in range(hops):
-        for way in range(2):
-            for e in range(4):
-                if e < 2 and (s or way == e):
-                    rs_copy(way, e, s).wait_send()
-                if s + 1 < hops or way == e // 2:
-                    g_copy(way, e, s + 1).wait_send()
-    for g in range(hops + 1):
-        p_copy(g).wait_send()
-        for o in range(1, nx):
-            x_copy(g, o).wait_send()
-        for o in range(1, members):
-            f_copy(g, o).wait_send()
+    all_sent(e_pair_in, p_ss.at[1])
+    all_sent(e_x_in.at[:, far_x], x_ss.at[1])
+    all_sent(f_in.at[:, others], f_ss.at[0])
+    finish(hops)
+    all_sent(e_f_in.at[:, others], f_ss.at[1])
 
 
 def hand_over(gram_in, scores_in, gram_ref, scores_ref):
@@ -465,17 +512,17 @@
             vmem((nx, 8, nq), f32),
             vmem((nx, 8, nq), f32),
             dma((3,)),
-            dma((members,)), dma((members,)),
-            dma((members,)), dma((members,)),
-            dma((2, 2, hops)), dma((2, 2, hops)),
-            dma((2, members)), dma((2, members)),
-            dma((members,)), dma((members,)),
-            dma((2, 4, hops)), dma((2, 4, hops)),
-            dma((hops + 1,)), dma((hops + 1,)),
-            dma((hops + 1, nx)), dma((hops + 1, nx)),
-            dma((hops + 1, members)), dma((hops + 1, members)),
+            dma((1,)), dma((members,)),
             dma((1,)), dma((1,)),
-            dma((nx,)), dma((nx,)),
+            dma((2, 2)), dma((2, 2, 2, hops)),
+            dma((1,)), dma((2, 2)),
+            dma((1,)), dma((2,)),
+            dma((2, 2)), dma((2, 4, hops)),
+            dma((2,)), dma((hops + 1,)),
+            dma((2,)), dma((hops + 1,)),
+            dma((2,)), dma((hops + 1,)),
+            dma((1,)), dma((1,)),
+            dma((1,)), dma((1,)),
         ],
         compiler_params=pltpu.CompilerParams(
             collective_id=0, has_side_effects=True, vmem_limit_bytes=56 * 1024 * 1024

time: 101 us -> 95.9 us (0.950)
  Pallas kernels: 99.8 us -> 95.1 us
    pallas_call x1, Pallas kernels: 98.2 us -> 93.6 us  [per_device(): pl.pallas_call(functools.partial(kernel, (ny, nz, nx, cl)), out_shape=(ja...]
where the time goes in v4:
time: 95.9 us; the launch traced here: 95.8 us
  Pallas kernels  95.1 us (99%)
    pallas_call x1, Pallas kernels, per_device(): pl.pallas_call(functools.partial(kernel, (ny, nz, nx, cl)), out_shape=(ja...  93.6 us

profile of v4, /device:TPU:1, one launch (start us, length us, event | category | flops | bytes accessed | tf_op | source)
XLA Modules:
  0.0 95.8 jit_solution(8159964888568716280)
XLA Ops:
  0.6 93.6 %shard_map.50 = (f32[8,4096]{1,0:T(8,128)}, f32[8,1024]{1,0:T(8,128)}) custom-call(bf16[512,1024]{1,0:T(8,128)(2,1)} %sk_ref.1, s32[1,512]{1,0:T(1,128)} %bitcast.1, bf16[1024,1024]{1,0:T(8,128)(2,1)} %qu_ref.1), custom_call_target="tpu_custom_call" | custom-call | tf_op jit(solution)/shard_map/pallas_call | solution.py:477
  94.2 1.6 %shard_map.51 = (f32[8,4096]{1,0:T(8,128)}, f32[8,1024]{1,0:T(8,128)}) custom-call(f32[8,4096]{1,0:T(8,128)} %get-tuple-element.4.gram_in, f32[8,1024]{1,0:T(8,128)} %get-tuple-element.5.scores_in), custom_call_target="tpu_custom_call" | custom-call | tf_op jit(solution)/shard_map/pallas_call | solution.py:531

commit v5 on v4

--- a/solution.py
+++ b/solution.py
@@ -119,7 +119,7 @@
 
     for o in range(1, members):
         ids_copy(o).start()
-    for o in range(1, members):
+    for o in [1, 3, 2, 5, 4, 7, 6]:
         docs_copy(o).start()
     own_quer = pltpu.make_async_copy(qu_ref, quer, local_sem.at[1])
     own_quer.start()
@@ -427,12 +427,13 @@
         if d == last:
             for g in waiting:
                 pair_sum(g)
+            for g in before:
+                x_sum(g)
     block(hops)
+    pair_sum(hops)
+    for g in waiting:
+        x_sum(g)
     before = before + waiting
-    for g in before[:-1]:
-        x_sum(g)
-    pair_sum(hops)
-    x_sum(before[-1])
     total = s_half[x]
     all_got(s_x_in.at[far_x], sx_rs.at[0])
     for o in range(1, nx):

time: 95.9 us -> 95.6 us (level)
  no operation moved by 1% of the time
where the time goes in v5:
time: 95.6 us; the launch traced here: 95.5 us
  Pallas kernels  94.9 us (99%)
    pallas_call x1, Pallas kernels, per_device(): pl.pallas_call(functools.partial(kernel, (ny, nz, nx, cl)), out_shape=(ja...  93.3 us

profile of v5, /device:TPU:1, one launch (start us, length us, event | category | flops | bytes accessed | tf_op | source)
XLA Modules:
  0.0 95.5 jit_solution(6768352075715128888)
XLA Ops:
  0.6 93.3 %shard_map.50 = (f32[8,4096]{1,0:T(8,128)}, f32[8,1024]{1,0:T(8,128)}) custom-call(bf16[512,1024]{1,0:T(8,128)(2,1)} %sk_ref.1, s32[1,512]{1,0:T(1,128)} %bitcast.1, bf16[1024,1024]{1,0:T(8,128)(2,1)} %qu_ref.1), custom_call_target="tpu_custom_call" | custom-call | tf_op jit(solution)/shard_map/pallas_call | solution.py:478
  93.9 1.6 %shard_map.51 = (f32[8,4096]{1,0:T(8,128)}, f32[8,1024]{1,0:T(8,128)}) custom-call(f32[8,4096]{1,0:T(8,128)} %get-tuple-element.4.gram_in, f32[8,1024]{1,0:T(8,128)} %get-tuple-element.5.scores_in), custom_call_target="tpu_custom_call" | custom-call | tf_op jit(solution)/shard_map/pallas_call | solution.py:532
